TPU v7x, 128 devices: a whole 4x4x4 slice. The times are simulated.
128 devices in a mesh: tm: 16 (over y, x_lo, core), tile: 8 (over x_hi, z).
Axes of the slice: x: 4 (x_hi: 2, x_lo: 2; x = x_hi * 2 + x_lo), y: 4, z: 4, core: 2. Of those that a mesh axis runs over, the one named last changes fastest.
Arguments:
- adjoint: bfloat16 [5120, 131072], P('tm', 'tile'), may hold values from -6 to 6
- emission: bfloat16 [5120, 131072], P('tm', 'tile'), may hold values from 0.29882812 to 3
- step_weights: float32 [5120], P('tm'), may hold values from 0.0041926275 to 0.041926276
- tile_list: int32 [4096, 2], P('tile'), may hold values from 0 to 1023, as said below
- counts: int32 [8], P('tile'), may hold values from 256 to 512, as said below
Outputs:
- coupling_grad: float32 [8, 512, 128, 128], P('tile', 'tm')
Inputs may be any that keep to these rules, and one draw needn't show every extreme that they name: Slot k of owner o is tile_list[o * 512 + k]; its row block lies in owner o's range o * 128 to (o + 1) * 128 - 1. For every owner and every other owner, the live slots of the first name exactly 4 distinct column blocks in the range of the second. The live slots of owner o are its first counts[o] slots; some owner has all 512 slots live.
All inputs are finite; a program needn't handle non-finite values.
Results may differ from a plain program's by a relative error of at most 0.009.
Values may be sent and summed in bfloat16 or wider, within the bound.
No kernel may reach another device: no remote copies, remote signals or barrier semaphores. Data moves between devices by JAX's collectives and lax.ppermute only.
A program may use at most 256 MiB of HBM per device.

v0:
```python
import math

import jax
import jax.numpy as jnp
from jax import lax
from jax.sharding import PartitionSpec as P

BLK = 128
CAP = 4


def body(adjoint, emission, step_weights, tile_list, counts):
    steps_here = adjoint.shape[0]
    owners = lax.axis_size("tile")
    own_blocks = adjoint.shape[1] // BLK
    my_owner = lax.axis_index("tile")
    weighted = (step_weights[:, None] * adjoint).astype(jnp.bfloat16)
    local_sums = jnp.sum(weighted.astype(jnp.float32) * emission.astype(jnp.float32), axis=0)
    slot_count = tile_list.shape[0]
    slot_ids = jnp.arange(slot_count, dtype=jnp.int32)
    live_slots = slot_ids < counts[0]
    row_local = tile_list[:, 0] - my_owner * own_blocks
    columns = tile_list[:, 1]
    source = columns // own_blocks
    within = columns % own_blocks
    owner_ids = jnp.arange(owners, dtype=jnp.int32)
    block_ids = jnp.arange(owners * own_blocks, dtype=jnp.int32)
    block_hits = jnp.any((columns[:, None] == block_ids[None, :]) & live_slots[:, None], axis=0)
    needed = (block_hits.reshape(owners, own_blocks) & (owner_ids[:, None] != my_owner)).astype(
        jnp.int32
    )
    all_tiles, all_counts = (
        lax.all_gather(tile_list, "tile", axis=0, tiled=True),
        lax.all_gather(counts, "tile", axis=0, tiled=True),
    )
    all_columns = all_tiles[:, 1].reshape(owners, slot_count)
    all_live = slot_ids[None, :] < all_counts[:, None]
    own_range = my_owner * own_blocks + jnp.arange(own_blocks, dtype=jnp.int32)
    asked_for = jnp.any(
        (all_columns[:, :, None] == own_range[None, None, :]) & all_live[:, :, None], axis=1
    )
    wanted = (asked_for & (owner_ids[:, None] != my_owner)).astype(jnp.int32)
    send_rank = jnp.cumsum(wanted, axis=1) - 1
    cap_ids = jnp.arange(CAP, dtype=jnp.int32)
    picked = (wanted[:, None, :] == 1) & (send_rank[:, None, :] == cap_ids[None, :, None])
    send_index = jnp.sum(
        picked.astype(jnp.int32) * jnp.arange(own_blocks, dtype=jnp.int32)[None, None, :], axis=2
    )
    emission_blocks = emission.reshape(steps_here, own_blocks, BLK)
    outgoing = jnp.take(emission_blocks, send_index.reshape(-1), axis=1).reshape(
        steps_here, owners, CAP, BLK
    )
    incoming = lax.all_to_all(outgoing, "tile", split_axis=1, concat_axis=1, tiled=True)
    column_table = jnp.concatenate(
        [emission_blocks, incoming.reshape(steps_here, owners * CAP, BLK)], axis=1
    )
    recv_rank = (jnp.cumsum(needed, axis=1) - 1).reshape(-1)
    slot_rank = jnp.clip(jnp.take(recv_rank, source * own_blocks + within), 0, CAP - 1)
    col_slot = jnp.where(source == my_owner, within, own_blocks + source * CAP + slot_rank)
    weighted_blocks = weighted.reshape(steps_here, own_blocks, BLK)
    tm_size = lax.axis_size("tm")
    tm_share = slot_count // tm_size
    group_size = math.gcd(tm_share * lax.axis_size("tm"), 128)

    def tile_group(index_pair):
        left_cols = jnp.take(weighted_blocks, index_pair[0], axis=1)
        right_cols = jnp.take(column_table, index_pair[1], axis=1)
        return jnp.einsum("sga,sgb->gab", left_cols, right_cols, preferred_element_type=jnp.float32)

    result = lax.map(
        tile_group, (row_local.reshape(-1, group_size), col_slot.reshape(-1, group_size))
    )
    result = result.reshape(tm_share * lax.axis_size("tm"), BLK, BLK)
    kept_tiles = lax.psum_scatter(result, "tm", scatter_dimension=0, tiled=True)
    first_slot = lax.axis_index("tm") * tm_share
    kept_rows = lax.dynamic_slice_in_dim(row_local, first_slot, tm_share)
    kept_live = lax.dynamic_slice_in_dim(live_slots, first_slot, tm_share)
    total_sums = lax.psum(local_sums, "tm")
    kept_tiles = (
        kept_tiles - jnp.take(total_sums.reshape(own_blocks, BLK), kept_rows, axis=0)[:, :, None]
    )
    kept_tiles = kept_tiles * kept_live.astype(jnp.float32)[:, None, None]
    return kept_tiles[None]


def solution(mesh):
    in_specs = (P("tm", "tile"), P("tm", "tile"), P("tm"), P("tile", None), P("tile"))
    out_specs = P("tile", "tm", None, None)
    return jax.shard_map(body, mesh=mesh, in_specs=in_specs, out_specs=out_specs, check_vma=False)
```

profile of v0, /device:TPU:0, one launch (start us, length us, event | category | flops | bytes accessed | tf_op | source)
XLA Modules:
  0.0 649.2 jit_solution(16105534542829298455)
XLA Ops:
  8.0 1.3 dynamic-slice.1
  9.3 0.8 dynamic-update-slice
  10.1 35.5 %all_gather.6 = s32[4096,2]{0,1:T(2,128)S(1)} all-gather(s32[512,2]{0,1:T(2,128)} %param.10), channel_id=1, replica_groups=mesh['tm'=16,'tile'=8] {'tile'}, dimensions={0}, use_global_device_ids=true | all-gather | bytes 36864 | tf_op jit(solution)/shard_map/all_gather | solution.py:33
  45.7 12.7 %all-reduce = s32[8]{0:T(128)S(1)} all-reduce(s32[8]{0:T(128)S(1)} %dynamic-update-slice), channel_id=1, replica_groups=mesh['tm'=16,'tile'=8] {'tile'}, use_global_device_ids=true, to_apply=%add | all-reduce | flops 8 | bytes 64
  58.9 1.4 and_reduce_fusion
  61.1 11.0 %copy_bitcast_fusion = bf16[320,128,128]{2,0,1:T(8,128)(2,1)} fusion(bf16[320,16384]{1,0:T(8,128)(2,1)} %param.8), kind=kLoop, calls=%fused_computation.30 | loop fusion | bytes 20971520 | tf_op jit(solution)/shard_map/reshape | solution.py:49
  72.1 5.0 gather_fusion.3
  77.1 1.8 broadcast_select_fusion
  78.9 3.6 all-to-all-start
  82.6 14.4 %multiply_reduce_fusion = (f32[16384]{0:T(1024)}, bf16[40,128,8,128]{3,2,1,0:T(8,128)(2,1)}) fusion(bf16[320,16384]{1,0:T(8,128)(2,1)} %param.8, bf16[320,16384]{1,0:T(8,128)(2,1)} %param.7, f32[320]{0:T(512)S(1)} %copy-done.1), kind=kLoop, calls=%fused_computation.27 | loop fusion | flops 36683776 | bytes 31524096 | tf_op jit(solution)/shard_map/reduce_sum | solution.py:18
  97.4 11.1 %copy.20 = bf16[40,8,128,128]{3,2,1,0:T(8,128)(2,1)} copy(bf16[40,8,128,128]{3,1,2,0:T(8,128)(2,1)} %bitcast.85) | data formatting | bytes 20971520
  108.5 10.9 %copy.23 = bf16[40,128,8,128]{3,2,0,1:T(8,128)(2,1)} copy(bf16[40,128,8,128]{3,2,1,0:T(8,128)(2,1)} %get-tuple-element.71) | data formatting | bytes 20971520 | tf_op jit(solution)/shard_map/reshape | solution.py:60
  119.4 2.5 gather_fusion.2
  121.9 2.0 copy.15
  123.9 6.0 pad_maximum_fusion
  130.0 15.6 %copy.17 = bf16[320,160,128]{2,0,1:T(8,128)(2,1)} copy(bf16[320,160,128]{2,1,0:T(8,128)(2,1)S(1)} %pad_maximum_fusion) | data formatting | bytes 26214400 | tf_op jit(solution)/shard_map/while | solution.py:70
  145.5 141.2 %while.10 = (s32[]{:T(128)}, f32[4,128,128,128]{3,2,1,0:T(8,128)}, s32[4,128]{1,0:T(4,128)S(1)}, bf16[320,128,128]{2,0,1:T(8,128)(2,1)}, s32[4,128]{1,0:T(4,128)S(1)}, /*index=5*/bf16[320,160,128]{2,0,1:T(8,128)(2,1)}, s32[]{:T(128)}) while((s32[]{:T(128)}, f32[4,128,128,128]{3,2,1,0:T(8,128)}, s32[4,128]{1,0:T(4,128)S(1)}, ...), condition=%wide.region_6.7_spmd, body=%wide.region_5.6_spmd.sunk | while | flops 1352667392 | bytes 71317088 | solution.py:70
  145.6 11.6 %gather_fusion.1 = bf16[128,320,128]{2,1,0:T(8,128)(2,1)} fusion(bf16[320,128,128]{2,0,1:T(8,128)(2,1)} %get-tuple-element.139, s32[1024]{0:T(1024)S(1)} %pad_clamp_fusion.8), kind=kCustom, calls=%fused_computation.clone.1 | custom fusion | bytes 20972032 | tf_op jit(solution)/shard_map/while/body/eval_jaxpr/jit(_take)/gather | solution.py:66
  157.2 12.2 %gather_fusion = bf16[128,320,128]{2,1,0:T(8,128)(2,1)} fusion(bf16[320,160,128]{2,0,1:T(8,128)(2,1)} %get-tuple-element.141, s32[1024]{0:T(1024)S(1)} %pad_clamp_fusion.7), kind=kCustom, calls=%fused_computation.1.clone.1 | custom fusion | bytes 20972032 | tf_op jit(solution)/shard_map/while/body/eval_jaxpr/jit(_take)/gather | solution.py:67
  169.4 11.4 %bitcast_dynamic-update-slice_fusion.2 = f32[4,128,128,128]{3,2,1,0:T(8,128)} fusion(f32[4,128,128,128]{3,2,1,0:T(8,128)} %get-tuple-element.130, s32[]{:T(128)S(6)} %copy.28, bf16[128,320,128]{2,1,0:T(8,128)(2,1)} %gather_fusion, pred[128]{0:T(512)(128)(4,1)S(1)} %get-tuple-element.119, bf16[128,320,128]{2,1,0:T(8,128)(2,1)} %gather_fusion.1, ...), kind=kOutput, calls=%fused_computation.12.clone.1 | convolution fusion | flops 1352663040 | bytes 29360388 | tf_op jit(solution)/shard_map/while/body/eval_jaxpr/sga,sgb->gab/dot_general | solution.py:68
  180.9 11.6 %gather_fusion.1 = bf16[128,320,128]{2,1,0:T(8,128)(2,1)} fusion(bf16[320,128,128]{2,0,1:T(8,128)(2,1)} %get-tuple-element.139, s32[1024]{0:T(1024)S(1)} %pad_clamp_fusion.8), kind=kCustom, calls=%fused_computation.clone.1 | custom fusion | bytes 20972032 | tf_op jit(solution)/shard_map/while/body/eval_jaxpr/jit(_take)/gather | solution.py:66
  192.5 12.2 %gather_fusion = bf16[128,320,128]{2,1,0:T(8,128)(2,1)} fusion(bf16[320,160,128]{2,0,1:T(8,128)(2,1)} %get-tuple-element.141, s32[1024]{0:T(1024)S(1)} %pad_clamp_fusion.7), kind=kCustom, calls=%fused_computation.1.clone.1 | custom fusion | bytes 20972032 | tf_op jit(solution)/shard_map/while/body/eval_jaxpr/jit(_take)/gather | solution.py:67
  204.7 11.4 %bitcast_dynamic-update-slice_fusion.2 = f32[4,128,128,128]{3,2,1,0:T(8,128)} fusion(f32[4,128,128,128]{3,2,1,0:T(8,128)} %get-tuple-element.130, s32[]{:T(128)S(6)} %copy.28, bf16[128,320,128]{2,1,0:T(8,128)(2,1)} %gather_fusion, pred[128]{0:T(512)(128)(4,1)S(1)} %get-tuple-element.119, bf16[128,320,128]{2,1,0:T(8,128)(2,1)} %gather_fusion.1, ...), kind=kOutput, calls=%fused_computation.12.clone.1 | convolution fusion | flops 1352663040 | bytes 29360388 | tf_op jit(solution)/shard_map/while/body/eval_jaxpr/sga,sgb->gab/dot_general | solution.py:68
  216.2 11.6 %gather_fusion.1 = bf16[128,320,128]{2,1,0:T(8,128)(2,1)} fusion(bf16[320,128,128]{2,0,1:T(8,128)(2,1)} %get-tuple-element.139, s32[1024]{0:T(1024)S(1)} %pad_clamp_fusion.8), kind=kCustom, calls=%fused_computation.clone.1 | custom fusion | bytes 20972032 | tf_op jit(solution)/shard_map/while/body/eval_jaxpr/jit(_take)/gather | solution.py:66
  227.8 12.2 %gather_fusion = bf16[128,320,128]{2,1,0:T(8,128)(2,1)} fusion(bf16[320,160,128]{2,0,1:T(8,128)(2,1)} %get-tuple-element.141, s32[1024]{0:T(1024)S(1)} %pad_clamp_fusion.7), kind=kCustom, calls=%fused_computation.1.clone.1 | custom fusion | bytes 20972032 | tf_op jit(solution)/shard_map/while/body/eval_jaxpr/jit(_take)/gather | solution.py:67
  240.0 11.4 %bitcast_dynamic-update-slice_fusion.2 = f32[4,128,128,128]{3,2,1,0:T(8,128)} fusion(f32[4,128,128,128]{3,2,1,0:T(8,128)} %get-tuple-element.130, s32[]{:T(128)S(6)} %copy.28, bf16[128,320,128]{2,1,0:T(8,128)(2,1)} %gather_fusion, pred[128]{0:T(512)(128)(4,1)S(1)} %get-tuple-element.119, bf16[128,320,128]{2,1,0:T(8,128)(2,1)} %gather_fusion.1, ...), kind=kOutput, calls=%fused_computation.12.clone.1 | convolution fusion | flops 1352663040 | bytes 29360388 | tf_op jit(solution)/shard_map/while/body/eval_jaxpr/sga,sgb->gab/dot_general | solution.py:68
  251.5 11.6 %gather_fusion.1 = bf16[128,320,128]{2,1,0:T(8,128)(2,1)} fusion(bf16[320,128,128]{2,0,1:T(8,128)(2,1)} %get-tuple-element.139, s32[1024]{0:T(1024)S(1)} %pad_clamp_fusion.8), kind=kCustom, calls=%fused_computation.clone.1 | custom fusion | bytes 20972032 | tf_op jit(solution)/shard_map/while/body/eval_jaxpr/jit(_take)/gather | solution.py:66
  263.1 12.2 %gather_fusion = bf16[128,320,128]{2,1,0:T(8,128)(2,1)} fusion(bf16[320,160,128]{2,0,1:T(8,128)(2,1)} %get-tuple-element.141, s32[1024]{0:T(1024)S(1)} %pad_clamp_fusion.7), kind=kCustom, calls=%fused_computation.1.clone.1 | custom fusion | bytes 20972032 | tf_op jit(solution)/shard_map/while/body/eval_jaxpr/jit(_take)/gather | solution.py:67
  275.3 11.4 %bitcast_dynamic-update-slice_fusion.2 = f32[4,128,128,128]{3,2,1,0:T(8,128)} fusion(f32[4,128,128,128]{3,2,1,0:T(8,128)} %get-tuple-element.130, s32[]{:T(128)S(6)} %copy.28, bf16[128,320,128]{2,1,0:T(8,128)(2,1)} %gather_fusion, pred[128]{0:T(512)(128)(4,1)S(1)} %get-tuple-element.119, bf16[128,320,128]{2,1,0:T(8,128)(2,1)} %gather_fusion.1, ...), kind=kOutput, calls=%fused_computation.12.clone.1 | convolution fusion | flops 1352663040 | bytes 29360388 | tf_op jit(solution)/shard_map/while/body/eval_jaxpr/sga,sgb->gab/dot_general | solution.py:68
  287.5 1.4 gather_fusion.4
  289.0 350.4 %reduce-scatter.2.cloned.1.call-done = f32[32,128,128]{2,1,0:T(8,128)} async-done(((f32[512,128,128]{2,1,0:T(8,128)}), f32[32,128,128]{2,1,0:T(8,128)}) %reduce-scatter.2.cloned.1.call-update) | async-done | bytes 2097168 | tf_op jit(solution)/shard_map/reduce_scatter | solution.py:74
  639.4 2.9 multiply_bitcast_fusion
  (59 shorter events, 3.5 us)
Async XLA Ops:
  7.2 53.9 %copy-start.2 = (pred[512]{0:T(512)(128)(4,1)}, pred[512]{0:T(512)(128)(4,1)S(1)}, u32[]{:S(2)}) copy-start(pred[512]{0:T(512)(128)(4,1)S(1)} %iota_compare_fusion.3) | copy-start | bytes 1540
  72.1 10.5 %copy-start.1 = (f32[320]{0:T(512)S(1)}, f32[320]{0:T(512)}, u32[]{:S(2)}) copy-start(f32[320]{0:T(512)} %param.9) | copy-start | bytes 3844
  78.9 43.0 %all-to-all-start = ((bf16[320,8,4,128]{3,0,2,1:T(8,128)(2,1)}), bf16[320,8,4,128]{3,0,2,1:T(8,128)(2,1)S(1)}, u32[]{:S(2)}, u32[]{:S(2)}) async-start(bf16[320,8,4,128]{3,0,2,1:T(8,128)(2,1)} %broadcast_select_fusion), calls=%async_computation | async-start | bytes 5242880 | tf_op jit(solution)/shard_map/all_to_all | solution.py:53
  82.5 204.9 %all-reduce.3.cloned.1.call-start = ((), (), s32[]{:S(2)}) async-start(), calls=%async_computation.3 | async-start | bytes 131072 | tf_op jit(solution)/shard_map/psum | solution.py:78
  97.0 542.4 %reduce-scatter.2.cloned.1.call-start = ((), (), s32[]{:S(2)}) async-start(), calls=%async_computation.2 | async-start | bytes 35651584 | tf_op jit(solution)/shard_map/reduce_scatter | solution.py:74
  108.5 10.9 %copy-start = (s32[512,2]{0,1:T(2,128)S(1)}, s32[512,2]{0,1:T(2,128)}, u32[]{:S(2)}) copy-start(s32[512,2]{0,1:T(2,128)} %param.10) | copy-start | bytes 12292
  286.7 0.6 copy-start.3
Sparse Core Ops, SparseCore 0:
  97.2 107.1 all-reduce.2
  286.8 352.5 reduce-scatter.1
where the time goes:
time: 650 us; the launch traced here: 649 us
  waiting for transfers between devices  350 us (54%)
  local copies, waits for them, and re-layouts  158 us (24%)
  blocking collectives  48.3 us (7%)
  matrix products  45.6 us (7%)
  other arithmetic  29.1 us (4%)
  between operations  14.2 us (2%)
    reduce_scatter x1, waiting for transfers between devices, body(): kept_tiles = lax.psum_scatter(result, 'tm', scatter_dimension=0, tiled=True)  350 us
    gather x4, local copies, waits for them, and re-layouts, tile_group(): right_cols = jnp.take(column_table, index_pair[1], axis=1)  48.9 us
    gather x4, local copies, waits for them, and re-layouts, tile_group(): left_cols = jnp.take(weighted_blocks, index_pair[0], axis=1)  46.4 us
    dot_general x4, matrix products, tile_group(): jnp.einsum('sga,sgb->gab', left_cols, right_cols, preferred_element_type=...  45.6 us
    all_gather x1, blocking collectives, body(): lax.all_gather(tile_list, 'tile', axis=0, tiled=True)  35.5 us
    while x1, local copies, waits for them, and re-layouts, body(): lax.map(tile_group, (row_local.reshape(-1, group_size), col_slot.reshape(...  15.6 us
    reduce_sum x1, other arithmetic, body(): jnp.sum(weighted.astype(jnp.float32) * emission.astype(jnp.float32), axis=0)  14.4 us
    unnamed x12, local copies, waits for them, and re-layouts  13.8 us
  transfers between devices with their start and end apart: 3, of which 1 were waited for; matrix products, arithmetic and copies ran while one was open for 32% of the time, Pallas kernels for 0%

commit v1 on v0

v1 whole, which is shorter than its diff:
```python
import functools

import jax
import jax.numpy as jnp
from jax import lax
from jax.experimental import pallas as pl
from jax.experimental.pallas import tpu as pltpu
from jax.sharding import PartitionSpec as P

BLK = 128
CAP = 4
GRP = 32
KA = 384
F32 = jnp.float32
BF16 = jnp.bfloat16
I32 = jnp.int32


def iota(shape, dim):
    return lax.broadcasted_iota(I32, shape, dim)


def plan_kernel(early, own_ref, count_ref, tiles_ref, request_ref, table_ref):
    slots = tiles_ref.shape[0]
    own = own_ref[0]
    r = tiles_ref[:, 0:1]
    c = tiles_ref[:, 1:2]
    k = iota((slots, 1), 0)
    src = c >> 7
    within = c & (BLK - 1)
    row = r & (BLK - 1)
    remote = (k < count_ref[0]) & (src != own)
    lane = iota((slots, BLK), 1)
    by_src = jnp.where((lane == src) & remote, 1.0, 0.0).astype(F32)
    by_block = jnp.where(lane == within, 1.0, 0.0).astype(F32)
    named = jnp.dot(by_src.T.astype(BF16), by_block.astype(BF16), preferred_element_type=F32)
    hit = jnp.where(named > 0.0, 1.0, 0.0).astype(F32)
    upper = jnp.where(iota((BLK, BLK), 0) <= iota((BLK, BLK), 1), 1.0, 0.0).astype(BF16)
    rank = jnp.dot(hit.astype(BF16), upper, preferred_element_type=F32) * hit
    slot_rank = jnp.sum(
        jnp.dot(by_src.astype(BF16), rank.astype(BF16), preferred_element_type=F32) * by_block,
        axis=1,
        keepdims=True,
    )
    slot_rank = jnp.clip(slot_rank.astype(I32) - 1, 0, CAP - 1)
    col = jnp.where(remote, BLK + src * CAP + slot_rank, within)

    jj = iota((slots, slots), 1)
    kk = iota((slots, slots), 0)
    same = (jj >> 5) == (kk >> 5)
    remote_f = jnp.broadcast_to(jnp.where(remote, 1.0, 0.0), (slots, BLK)).astype(BF16)
    ahead = jnp.where(same & (jj < kk), 1.0, 0.0).astype(BF16)
    ahead = jnp.dot(ahead, remote_f, preferred_element_type=F32)[:, 0:1].astype(I32)
    total = jnp.where(same, 1.0, 0.0).astype(BF16)
    total = jnp.dot(total, remote_f, preferred_element_type=F32)[:, 0:1].astype(I32)
    s = k & (GRP - 1)
    pos = jnp.where(remote, GRP - total + ahead, s - ahead)
    value = jnp.where(lane < GRP, row, jnp.where(lane < 2 * GRP, col, s))
    value = jnp.where((lane & (GRP - 1)) == pos, value, 0)
    value = jnp.where(lane < 3 * GRP, value, 0).astype(F32).astype(BF16)
    groups = slots // GRP
    pick = jnp.where((iota((groups, slots), 1) >> 5) == iota((groups, slots), 0), 1.0, 0.0)
    table_ref[...] = jnp.dot(pick.astype(BF16), value, preferred_element_type=F32).astype(I32)

    late = jnp.max(jnp.where(total > GRP - early, 1, 0), axis=0, keepdims=True)
    owners = request_ref.shape[0]
    hit8 = hit[0:owners, :]
    rank8 = rank[0:owners, :]
    lane8 = iota((owners, BLK), 1)
    request = jnp.where(lane8 == CAP, jnp.broadcast_to(late, (owners, BLK)), 0)
    for q in range(CAP):
        block = jnp.sum(
            jnp.where((rank8 == q + 1.0) & (hit8 > 0.0), lane8, 0), axis=1, keepdims=True
        )
        request = jnp.where(lane8 == q, block, request)
    request_ref[...] = request


def plan(own, counts, tile_list, owners, early):
    slots = tile_list.shape[0]
    smem = pl.BlockSpec(memory_space=pltpu.SMEM)
    vmem = pl.BlockSpec(memory_space=pltpu.VMEM)
    return pl.pallas_call(
        functools.partial(plan_kernel, early),
        in_specs=[smem, smem, vmem],
        out_specs=[vmem, vmem],
        out_shape=[
            jax.ShapeDtypeStruct((owners, BLK), I32),
            jax.ShapeDtypeStruct((slots // GRP, BLK), I32),
        ],
        compiler_params=pltpu.CompilerParams(vmem_limit_bytes=16 * 2**20),
        name="plan",
    )(own, counts, tile_list)


STEP = 16
DEPTH = 3


def prep_kernel(weights_ref, adj_ref, em_ref, wt_ref, e_ref, abuf, ebuf, wide, asem, esem):
    steps = adj_ref.shape[0]
    blocks = e_ref.shape[0]
    chunks = blocks // STEP
    wide[...] = jnp.broadcast_to(weights_ref[...], wide.shape)

    def copies(j):
        slot = lax.rem(j, DEPTH)
        cols = pl.ds(pl.multiple_of(j * (STEP * BLK), STEP * BLK), STEP * BLK)
        return (
            pltpu.make_async_copy(adj_ref.at[:, cols], abuf.at[slot], asem.at[slot]),
            pltpu.make_async_copy(em_ref.at[:, cols], ebuf.at[slot], esem.at[slot]),
        )

    for j in range(DEPTH - 1):
        for copy in copies(j):
            copy.start()
    ones = jnp.where(iota((KA - steps, BLK), 0) < 2, 1.0, 0.0).astype(BF16)
    rows = iota((KA - steps, BLK), 0)

    def chunk(j, carry):
        slot = lax.rem(j, DEPTH)

        @pl.when(j + DEPTH - 1 < chunks)
        def _():
            for copy in copies(j + DEPTH - 1):
                copy.start()

        for copy in copies(j):
            copy.wait()

        def some(i, inner):
            for b in range(4):
                cols = pl.ds(pl.multiple_of((i * 4 + b) * BLK, BLK), BLK)
                at = j * STEP + i * 4 + b
                w = (wide[...] * abuf[slot, :, cols].astype(F32)).astype(BF16)
                e = ebuf[slot, :, cols]
                sums = -jnp.sum(w.astype(F32) * e.astype(F32), axis=0, keepdims=True)
                high = sums.astype(BF16).astype(F32)
                low = sums - high
                tail = jnp.where(rows == 0, high, jnp.where(rows == 1, low, 0.0)).astype(BF16)
                wt_ref[at] = jnp.concatenate([w, tail], axis=0).T
                e_ref[at, 0:steps, :] = e
                e_ref[at, steps:KA, :] = ones
            return inner

        lax.fori_loop(0, STEP // 4, some, 0)
        return carry

    lax.fori_loop(0, chunks, chunk, 0)


def prep(weights, adjoint, emission):
    steps, nodes = adjoint.shape
    blocks = nodes // BLK
    anyspace = pl.BlockSpec(memory_space=pl.ANY)
    vmem = pl.BlockSpec(memory_space=pltpu.VMEM)
    return pl.pallas_call(
        prep_kernel,
        in_specs=[vmem, anyspace, anyspace],
        out_specs=[vmem, vmem],
        out_shape=[
            pltpu.VMEM((blocks, BLK, KA), BF16),
            pltpu.VMEM((blocks, KA, BLK), BF16),
        ],
        scratch_shapes=[
            pltpu.VMEM((DEPTH, steps, STEP * BLK), BF16),
            pltpu.VMEM((DEPTH, steps, STEP * BLK), BF16),
            pltpu.VMEM((steps, BLK), F32),
            pltpu.SemaphoreType.DMA((DEPTH,)),
            pltpu.SemaphoreType.DMA((DEPTH,)),
        ],
        compiler_params=pltpu.CompilerParams(vmem_limit_bytes=14 * 2**20),
        cost_estimate=pl.CostEstimate(
            flops=4 * steps * nodes, bytes_accessed=8 * steps * nodes, transcendentals=0
        ),
        name="prep",
    )(weights, adjoint, emission)


def pack_kernel(asked_ref, em_ref, out_ref, sems):
    count = out_ref.shape[0]

    def copy(i):
        block = asked_ref[i >> 2, i & (CAP - 1)] & (BLK - 1)
        cols = pl.ds(pl.multiple_of(block * BLK, BLK), BLK)
        return pltpu.make_async_copy(em_ref.at[:, cols], out_ref.at[i], sems.at[i])

    for i in range(count):
        copy(i).start()
    for i in range(count):
        copy(i).wait()


def pack(asked, emission):
    owners = asked.shape[0]
    smem = pl.BlockSpec(memory_space=pltpu.SMEM)
    anyspace = pl.BlockSpec(memory_space=pl.ANY)
    return pl.pallas_call(
        pack_kernel,
        in_specs=[smem, anyspace],
        out_specs=anyspace,
        out_shape=jax.ShapeDtypeStruct((owners * CAP, emission.shape[0], BLK), BF16),
        scratch_shapes=[pltpu.SemaphoreType.DMA((owners * CAP,))],
        compiler_params=pltpu.CompilerParams(vmem_limit_bytes=4 * 2**20),
        name="pack",
    )(asked, emission)


def tiles_kernel(ranges, runs, base, per, with_add, *refs):
    groups_ref, places_ref, table_ref, wt_ref, e_ref, far_ref = refs[:6]
    refs = refs[6:]
    add_ref = None
    if with_add:
        add_ref, refs = refs[0], refs[1:]
    outs, (far, sem) = refs[: len(ranges)], refs[len(ranges) :]
    steps = far_ref.shape[1]
    copy = pltpu.make_async_copy(far_ref, far.at[:, pl.ds(0, steps)], sem)
    copy.start()
    ones = jnp.where(iota((KA - steps, BLK), 0) < 2, 1.0, 0.0).astype(BF16)

    def fill(i, carry):
        far[i, steps:KA, :] = ones
        return carry

    lax.fori_loop(0, far.shape[0], fill, 0)

    def put(out_ref, at, n, p, acc):
        if with_add:
            acc = acc + add_ref[places_ref[n] * per + (p - base)].astype(F32)
        out_ref[at] = acc.astype(BF16)

    n0 = 0
    for out_ref, (first, count), run in zip(outs, ranges, runs):
        total = out_ref.shape[0] // count

        def near(i, carry, out_ref=out_ref, first=first, count=count, run=run, n0=n0):
            for j in range(run):
                g = groups_ref[n0 + i * run + j]
                for q in range(count):
                    row = table_ref[g, first + q]
                    col = jnp.minimum(table_ref[g, GRP + first + q], BLK - 1)
                    acc = jnp.dot(wt_ref[row], e_ref[col], preferred_element_type=F32)
                    put(out_ref, (i * run + j) * count + q, n0 + i * run + j, first + q, acc)
            return carry

        lax.fori_loop(0, total // run, near, 0)
        n0 += total
    copy.wait()
    n0 = 0
    for out_ref, (first, count) in zip(outs, ranges):
        total = out_ref.shape[0] // count

        def distant(i, carry, out_ref=out_ref, first=first, count=count, n0=n0):
            n = n0 + i // count
            p = first + lax.rem(i, count)
            g = groups_ref[n]
            col = table_ref[g, GRP + p]

            @pl.when(col >= BLK)
            def _():
                row = table_ref[g, p]
                acc = jnp.dot(wt_ref[row], far[col - BLK], preferred_element_type=F32)
                put(out_ref, i, n, p, acc)

            return carry

        lax.fori_loop(0, out_ref.shape[0], distant, 0)
        n0 += total


def tiles(groups, places, table, wt, e_blocks, far, ranges, sizes, runs, base, per, add=None):
    smem = pl.BlockSpec(memory_space=pltpu.SMEM)
    vmem = pl.BlockSpec(memory_space=pltpu.VMEM)
    counts = [size * count for size, (_, count) in zip(sizes, ranges)]
    return pl.pallas_call(
        functools.partial(tiles_kernel, ranges, runs, base, per, add is not None),
        in_specs=[smem, smem, smem, vmem, vmem, pl.BlockSpec(memory_space=pl.ANY)]
        + ([vmem] if add is not None else []),
        out_specs=[vmem] * len(counts),
        out_shape=[jax.ShapeDtypeStruct((c, BLK, BLK), BF16) for c in counts],
        scratch_shapes=[pltpu.VMEM((far.shape[0], KA, BLK), BF16), pltpu.SemaphoreType.DMA],
        compiler_params=pltpu.CompilerParams(vmem_limit_bytes=24 * 2**20),
        cost_estimate=pl.CostEstimate(
            flops=4 * sum(counts) * BLK * BLK * KA,
            bytes_accessed=2 * sum(counts) * BLK * BLK,
            transcendentals=0,
        ),
        name="tiles",
    )(groups, places, table, wt, e_blocks, far, *([add] if add is not None else []))


def add_kernel(n, *refs):
    for i in range(n):
        mine, came = refs[2 * i], refs[2 * i + 1]
        sent, kept = refs[2 * n + 2 * i], refs[2 * n + 2 * i + 1]
        half = sent.shape[0]

        def one(j, carry, mine=mine, came=came, sent=sent, kept=kept, half=half):
            sent[j] = (mine[j].astype(F32) + came[j].astype(F32)).astype(BF16)
            kept[j] = (mine[half + j].astype(F32) + came[half + j].astype(F32)).astype(BF16)
            return carry

        lax.fori_loop(0, half, one, 0, unroll=2)


def add_pairs(pairs):
    vmem = pl.BlockSpec(memory_space=pltpu.VMEM)
    shapes = []
    for mine, _ in pairs:
        shapes += [jax.ShapeDtypeStruct((mine.shape[0] // 2, BLK, BLK), BF16)] * 2
    flat = [a for pair in pairs for a in pair]
    size = sum(a.size for a in flat)
    return pl.pallas_call(
        functools.partial(add_kernel, len(pairs)),
        in_specs=[vmem] * len(flat),
        out_specs=[vmem] * len(shapes),
        out_shape=shapes,
        compiler_params=pltpu.CompilerParams(vmem_limit_bytes=20 * 2**20),
        cost_estimate=pl.CostEstimate(flops=size, bytes_accessed=3 * size, transcendentals=0),
        name="add_pairs",
    )(*flat)


def finish_kernel(firsts, me_ref, count_ref, table_ref, *refs):
    me = me_ref[0]
    out_ref = refs[-1]
    for i, first in enumerate(firsts):
        mine, came = refs[2 * i], refs[2 * i + 1]

        def one(j, carry, mine=mine, came=came, first=first):
            s = table_ref[me, 2 * GRP + first + j]
            live = jnp.where(me * GRP + s < count_ref[0], 1.0, 0.0).astype(F32)
            out_ref[s] = (mine[j].astype(F32) + came[j].astype(F32)) * live
            return carry

        lax.fori_loop(0, mine.shape[0], one, 0)


def finish(me, counts, table, firsts, pairs):
    smem = pl.BlockSpec(memory_space=pltpu.SMEM)
    vmem = pl.BlockSpec(memory_space=pltpu.VMEM)
    flat = [a for pair in pairs for a in pair]
    return pl.pallas_call(
        functools.partial(finish_kernel, firsts),
        in_specs=[smem, smem, smem] + [vmem] * len(flat),
        out_specs=vmem,
        out_shape=jax.ShapeDtypeStruct((GRP, BLK, BLK), F32),
        compiler_params=pltpu.CompilerParams(vmem_limit_bytes=16 * 2**20),
        name="finish",
    )(me, counts, table, *flat)


CORE, ALONG_X, UP_Y, DOWN_Y = 1, 2, 4, 12
ORDERS = (
    (ALONG_X, UP_Y, DOWN_Y),
    (UP_Y, DOWN_Y, ALONG_X),
    (DOWN_Y, ALONG_X, UP_Y),
)


def swap(a, mask):
    n = lax.axis_size("tm")
    return lax.ppermute(a, "tm", [(i, i ^ mask) for i in range(n)])


def order_masks(order, lead):
    first, second, third = order
    return [lead * first ^ s * second ^ t * third for s in (1, 0) for t in (1, 0)]


def body(adjoint, emission, step_weights, tile_list, counts):
    owners = lax.axis_size("tile")
    parts = lax.axis_size("tm")
    own = lax.axis_index("tile").astype(I32).reshape(1)
    me = lax.axis_index("tm").astype(I32).reshape(1)
    request, table = plan(own, counts, tile_list, owners, GRP)
    asked = lax.all_to_all(request, "tile", split_axis=0, concat_axis=0, tiled=True)
    outgoing = pack(asked, emission)
    far = lax.all_to_all(outgoing, "tile", split_axis=0, concat_axis=0, tiled=True)
    outgoing, step_weights = lax.optimization_barrier((outgoing, step_weights))
    wt, e_blocks = prep(step_weights[:, None], adjoint, emission)
    wt = pltpu.with_memory_space_constraint(wt, pltpu.VMEM)
    e_blocks = pltpu.with_memory_space_constraint(e_blocks, pltpu.VMEM)

    half = GRP // 2
    cuts = (6, 5, 5)
    others = me ^ CORE ^ (2 * jnp.arange(parts // 2, dtype=I32))
    masks = [m for order in ORDERS for lead in (1, 0) for m in order_masks(order, lead)]
    mine = me ^ jnp.array(masks, I32)
    places = jnp.array([m // 2 for m in masks], I32)
    sent = []
    for c in range(2):
        (s,) = tiles(
            others, places, table, wt, e_blocks, far, ((c * half, half),), (8,), (1,), c * half, half
        )
        sent.append(s)
    came = [swap(s, CORE) for s in sent]
    pairs, firsts = [], []
    for c in range(2):
        ranges, first = [], c * half
        for n in cuts:
            ranges += [(first, n), (first, n)]
            firsts.append(first)
            first += n
        out = tiles(
            mine, places, table, wt, e_blocks, far,
            tuple(ranges), (4,) * 6, (2,) * 6, c * half, half, came[c],
        )
        for step in range(2):
            now = [
                (out[2 * i + 1], swap(out[2 * i], order[step])) for i, order in enumerate(ORDERS)
            ]
            out = add_pairs(now)
        pairs += [(out[2 * i + 1], swap(out[2 * i], order[2])) for i, order in enumerate(ORDERS)]
    return finish(me, counts, table, tuple(firsts), pairs)[None]


def solution(mesh):
    in_specs = (P("tm", "tile"), P("tm", "tile"), P("tm"), P("tile", None), P("tile"))
    out_specs = P("tile", "tm", None, None)
    return jax.shard_map(body, mesh=mesh, in_specs=in_specs, out_specs=out_specs, check_vma=False)
```

time: 650 us -> 181 us (0.28)
  waiting for transfers between devices: 350 us -> 30.4 us
  local copies, waits for them, and re-layouts: 158 us -> 31.5 us
  Pallas kernels: 0 us -> 74.8 us
  matrix products: 45.6 us -> 0 us
  blocking collectives: 48.3 us -> 15.3 us
  other arithmetic: 29.1 us -> 0.01 us
  starting transfers between devices: 3.71 us -> 26.8 us
  between operations: 14.2 us -> 0.86 us
    reduce_scatter x1 -> x0, waiting for transfers between devices: 350 us -> none  [body(): kept_tiles = lax.psum_scatter(result, 'tm', scatter_dimension=0, tiled=True)]
    gather x11 -> x0, local copies, waits for them, and re-layouts: 104 us -> none  [the longest x4 48.9 us: tile_group(): right_cols = jnp.take(column_table, index_pair[1], axis=1)]
    pallas_call x0 -> x12, Pallas kernels: none -> 74.8 us  [the longest x4 54.6 us: tiles(): pl.pallas_call(functools.partial(tiles_kernel, ranges, runs, base, per, a...]
    dot_general x4 -> x0, matrix products: 45.6 us -> none  [tile_group(): jnp.einsum('sga,sgb->gab', left_cols, right_cols, preferred_element_type=...]
    all_gather x1 -> x0, blocking collectives: 35.5 us -> none  [body(): lax.all_gather(tile_list, 'tile', axis=0, tiled=True)]
    ppermute x0 -> x20, waiting for transfers between devices: none -> 25.5 us  [swap(): return lax.ppermute(a, 'tm', [(i, i ^ mask) for i in range(n)])]
    ppermute x0 -> x20, starting transfers between devices: none -> 23.1 us  [swap(): return lax.ppermute(a, 'tm', [(i, i ^ mask) for i in range(n)])]
    reshape x3 -> x0, local copies, waits for them, and re-layouts: 21.9 us -> none  [the longest x1 11 us: body(): emission_blocks = emission.reshape(steps_here, own_blocks, BLK)]
  transfers between devices with their start and end apart: 3 -> 21, of which waited for: 1 -> 10; matrix products, arithmetic and copies ran while one was open for 32% -> 0% of each run, Pallas kernels for 0% -> 30%
where the time goes in v1:
time: 181 us; the launch traced here: 180 us
  Pallas kernels  74.8 us (41%)
  local copies, waits for them, and re-layouts  31.5 us (17%)
  waiting for transfers between devices  30.4 us (17%)
  starting transfers between devices  26.8 us (15%)
  blocking collectives  15.3 us (8%)
    pallas_call x4, Pallas kernels, tiles(): pl.pallas_call(functools.partial(tiles_kernel, ranges, runs, base, per, a...  54.6 us
    unnamed x25, local copies, waits for them, and re-layouts  31.4 us
    ppermute x20, waiting for transfers between devices, swap(): return lax.ppermute(a, 'tm', [(i, i ^ mask) for i in range(n)])  25.5 us
    ppermute x20, starting transfers between devices, swap(): return lax.ppermute(a, 'tm', [(i, i ^ mask) for i in range(n)])  23.1 us
    all_to_all x1, blocking collectives, body(): lax.all_to_all(request, 'tile', split_axis=0, concat_axis=0, tiled=True)  15.3 us
    pallas_call x1, Pallas kernels, prep(): pl.pallas_call(prep_kernel, in_specs=[vmem, anyspace, anyspace], out_spec...  12.7 us
    all_to_all x1, waiting for transfers between devices, body(): lax.all_to_all(outgoing, 'tile', split_axis=0, concat_axis=0, tiled=True)  4.87 us
    all_to_all x1, starting transfers between devices, body(): lax.all_to_all(outgoing, 'tile', split_axis=0, concat_axis=0, tiled=True)  3.76 us
  transfers between devices with their start and end apart: 21, of which 10 were waited for; matrix products, arithmetic and copies ran while one was open for 0% of the time, Pallas kernels for 30%

profile of v1, /device:TPU:0, one launch (start us, length us, event | category | flops | bytes accessed | tf_op | source)
XLA Modules:
  0.0 179.7 jit_solution(6039737185603157000)
XLA Ops:
  1.5 1.6 plan.1
  3.0 15.3 %all_to_all.16 = s32[8,1,128]{2,1,0:T(1,128)S(1)} all-to-all(s32[8,1,128]{2,1,0:T(1,128)S(1)} %bitcast.9), channel_id=1, replica_groups=mesh['tm'=16,'tile'=8] {'tile'}, dimensions={0} | all-to-all | bytes 8192 | tf_op jit(solution)/shard_map/all_to_all | solution.py:377
  18.4 4.0 %copy-done.5 = bf16[320,16384]{1,0:T(8,128)(2,1)S(1)} copy-done((bf16[320,16384]{1,0:T(8,128)(2,1)S(1)}, bf16[320,16384]{1,0:T(8,128)(2,1)}, u32[]{:S(2)}) %copy-start.5) | copy-done | bytes 10485784
  22.3 1.8 %pack.1 = bf16[32,320,128]{2,1,0:T(8,128)(2,1)S(1)} custom-call(s32[8,128]{1,0:T(8,128)S(1)} %bitcast.8, bf16[320,16384]{1,0:T(8,128)(2,1)S(1)} %copy-done.5), custom_call_target="tpu_custom_call" | custom-call | tf_op jit(solution)/shard_map/pack/pallas_call | solution.py:198
  24.2 1.5 copy-done.7
  25.7 3.8 %all-to-all-start.1 = ((bf16[32,320,128]{2,1,0:T(8,128)(2,1)}), bf16[32,320,128]{2,1,0:T(8,128)(2,1)S(1)}, u32[]{:S(2)}, u32[]{:S(2)}) async-start(bf16[32,320,128]{2,1,0:T(8,128)(2,1)} %copy-done.7), calls=%async_computation.1 | async-start | bytes 5242880 | tf_op jit(solution)/shard_map/all_to_all | solution.py:379
  29.6 4.0 %copy-done.6 = bf16[320,16384]{1,0:T(8,128)(2,1)S(1)} copy-done((bf16[320,16384]{1,0:T(8,128)(2,1)S(1)}, bf16[320,16384]{1,0:T(8,128)(2,1)}, u32[]{:S(2)}) %copy-start.6) | copy-done | bytes 10485784
  33.6 12.7 %prep.1 = (bf16[128,128,384]{2,1,0:T(8,128)(2,1)S(1)}, bf16[128,384,128]{2,1,0:T(8,128)(2,1)S(1)}) custom-call(f32[320,1]{1,0:T(8,128)S(1)} %broadcast_in_dim.8.weights_ref, bf16[320,16384]{1,0:T(8,128)(2,1)S(1)} %copy-done.6, bf16[320,16384]{1,0:T(8,128)(2,1)} %em_ref.3), custom_call_target="tpu_custom_call" | custom-call | flops 20971520 | bytes 41943040 | tf_op jit(solution)/shard_map/prep/pallas_call | solution.py:157
  46.3 4.5 %copy-done = bf16[128,128,384]{2,1,0:T(8,128)(2,1)} copy-done((bf16[128,128,384]{2,1,0:T(8,128)(2,1)}, bf16[128,128,384]{2,1,0:T(8,128)(2,1)S(1)}, u32[]{:S(2)}) %copy-start) | copy-done | bytes 12582936
  50.8 4.5 %copy-done.2 = bf16[128,384,128]{2,1,0:T(8,128)(2,1)} copy-done((bf16[128,384,128]{2,1,0:T(8,128)(2,1)}, bf16[128,384,128]{2,1,0:T(8,128)(2,1)S(1)}, u32[]{:S(2)}) %copy-start.2) | copy-done | bytes 12582936
  55.4 4.9 %all-to-all-done.1.refs_5_ = bf16[32,320,128]{2,1,0:T(8,128)(2,1)S(1)} async-done(((bf16[32,320,128]{2,1,0:T(8,128)(2,1)}), bf16[32,320,128]{2,1,0:T(8,128)(2,1)S(1)}, u32[]{:S(2)}, u32[]{:S(2)}) %all-to-all-start.1) | async-done | bytes 2621472 | tf_op jit(solution)/shard_map/all_to_all | solution.py:379
  60.3 5.5 %copy-done.1 = bf16[128,128,384]{2,1,0:T(8,128)(2,1)S(1)} copy-done((bf16[128,128,384]{2,1,0:T(8,128)(2,1)S(1)}, bf16[128,128,384]{2,1,0:T(8,128)(2,1)}, u32[]{:S(2)}) %copy-start.1) | copy-done | bytes 12582936
  65.8 4.6 %copy-done.3 = bf16[128,384,128]{2,1,0:T(8,128)(2,1)S(1)} copy-done((bf16[128,384,128]{2,1,0:T(8,128)(2,1)S(1)}, bf16[128,384,128]{2,1,0:T(8,128)(2,1)}, u32[]{:S(2)}) %copy-start.3) | copy-done | bytes 12582936
  70.3 15.7 %tiles.6 = bf16[128,128,128]{2,1,0:T(8,128)(2,1)} custom-call(s32[8]{0:T(128)S(1)} %multiply_xor_fusion.refs_0_, s32[24]{0:T(128)S(1)} %copy-done.8, s32[16,128]{1,0:T(8,128)S(1)} %get-tuple-element.46.refs_2_.table_ref, bf16[128,128,384]{2,1,0:T(8,128)(2,1)S(1)} %copy-done.1, bf16[128,384,128]{2,1,0:T(8,128)(2,1)S(1)} %copy-done.3, ...), custom_call_target="tpu_custom_call" | custom-call | flops 3221225472 | bytes 4194304 | tf_op jit(solution)/shard_map/tiles/pallas_call | solution.py:275
  86.2 11.0 %tiles.4 = bf16[128,128,128]{2,1,0:T(8,128)(2,1)} custom-call(s32[8]{0:T(128)S(1)} %multiply_xor_fusion.refs_0_, s32[24]{0:T(128)S(1)} %copy-done.8, s32[16,128]{1,0:T(8,128)S(1)} %get-tuple-element.46.refs_2_.table_ref, bf16[128,128,384]{2,1,0:T(8,128)(2,1)S(1)} %copy-done.1, bf16[128,384,128]{2,1,0:T(8,128)(2,1)S(1)} %copy-done.3, ...), custom_call_target="tpu_custom_call" | custom-call | flops 3221225472 | bytes 4194304 | tf_op jit(solution)/shard_map/tiles/pallas_call | solution.py:275
  97.8 16.3 %tiles.7 = (bf16[24,128,128]{2,1,0:T(8,128)(2,1)S(1)}, bf16[24,128,128]{2,1,0:T(8,128)(2,1)S(1)}, bf16[20,128,128]{2,1,0:T(8,128)(2,1)S(1)}, bf16[20,128,128]{2,...) custom-call(s32[24]{0:T(128)S(1)} %broadcast_xor_fusion.refs_0_, ...), custom_call_target="tpu_custom_call" | custom-call | flops 3221225472 | bytes 4194304 | tf_op jit(solution)/shard_map/tiles/pallas_call | solution.py:275
  114.1 1.7 collective-permute-start.12
  116.3 2.2 %collective-permute-start.13 = (bf16[20,128,128]{2,1,0:T(8,128)(2,1)S(1)}, bf16[20,128,128]{2,1,0:T(8,128)(2,1)S(1)}, u32[]{:S(2)}, u32[]{:S(2)}) collective-permute-start(bf16[20,128,128]{2,1,0:T(8,128)(2,1)S(1)} %get-tuple-element.74), channel_id=1, source_target_pairs={{0,96},{8,104},{16,112},{24,120},{32,64},{40,72},{48,80},{56,88},{... | collective-permute-start | bytes 1966088 | tf_op jit(solution)/shard_map/ppermute | solution.py:363
  118.5 2.0 %copy-done.9 = bf16[128,128,128]{2,1,0:T(8,128)(2,1)} copy-done((bf16[128,128,128]{2,1,0:T(8,128)(2,1)}, bf16[128,128,128]{2,1,0:T(8,128)(2,1)S(1)}, u32[]{:S(2)}) %copy-start.9) | copy-done | bytes 4194328
  120.5 11.6 %tiles.5 = (bf16[24,128,128]{2,1,0:T(8,128)(2,1)S(1)}, bf16[24,128,128]{2,1,0:T(8,128)(2,1)S(1)}, bf16[20,128,128]{2,1,0:T(8,128)(2,1)S(1)}, bf16[20,128,128]{2,...) custom-call(s32[24]{0:T(128)S(1)} %broadcast_xor_fusion.refs_0_, ...), custom_call_target="tpu_custom_call" | custom-call | flops 3221225472 | bytes 4194304 | tf_op jit(solution)/shard_map/tiles/pallas_call | solution.py:275
  132.1 1.7 collective-permute-start.1
  136.2 2.8 %collective-permute-start.15 = (bf16[10,128,128]{2,1,0:T(8,128)(2,1)S(1)}, bf16[10,128,128]{2,1,0:T(8,128)(2,1)S(1)}, u32[]{:S(2)}, u32[]{:S(2)}) collective-permute-start(bf16[10,128,128]{2,1,0:T(8,128)(2,1)S(1)} %get-tuple-element.78), channel_id=1, source_target_pairs={{0,96},{8,104},{16,112},{24,120},{32,64},{40,72},{48,80},{56,88},{... | collective-permute-start | bytes 983048 | tf_op jit(solution)/shard_map/ppermute | solution.py:363
  139.6 11.8 %collective-permute-done.2.refs_3_ = bf16[20,128,128]{2,1,0:T(8,128)(2,1)S(1)} collective-permute-done((bf16[20,128,128]{2,1,0:T(8,128)(2,1)S(1)}, bf16[20,128,128]{2,1,0:T(8,128)(2,1)S(1)}, u32[]{:S(2)}, u32[]{:S(2)}) %collective-permute-start.2) | collective-permute-done | bytes 655392 | tf_op jit(solution)/shard_map/ppermute | solution.py:363
  152.0 1.3 collective-permute-done.3.refs_5_
  154.1 3.0 %collective-permute-start.5 = (bf16[10,128,128]{2,1,0:T(8,128)(2,1)S(1)}, bf16[10,128,128]{2,1,0:T(8,128)(2,1)S(1)}, u32[]{:S(2)}, u32[]{:S(2)}) collective-permute-start(bf16[10,128,128]{2,1,0:T(8,128)(2,1)S(1)} %get-tuple-element.60), channel_id=1, source_target_pairs={{0,96},{8,104},{16,112},{24,120},{32,64},{40,72},{48,80},{56,88},{... | collective-permute-start | bytes 983048 | tf_op jit(solution)/shard_map/ppermute | solution.py:363
  157.1 3.2 %collective-permute-done.15.refs_3_ = bf16[10,128,128]{2,1,0:T(8,128)(2,1)S(1)} collective-permute-done((bf16[10,128,128]{2,1,0:T(8,128)(2,1)S(1)}, bf16[10,128,128]{2,1,0:T(8,128)(2,1)S(1)}, u32[]{:S(2)}, u32[]{:S(2)}) %collective-permute-start.15) | collective-permute-done | bytes 327712 | tf_op jit(solution)/shard_map/ppermute | solution.py:363
  161.2 1.5 collective-permute-start.18
  163.4 3.7 %collective-permute-done.5.refs_3_ = bf16[10,128,128]{2,1,0:T(8,128)(2,1)S(1)} collective-permute-done((bf16[10,128,128]{2,1,0:T(8,128)(2,1)S(1)}, bf16[10,128,128]{2,1,0:T(8,128)(2,1)S(1)}, u32[]{:S(2)}, u32[]{:S(2)}) %collective-permute-start.5) | collective-permute-done | bytes 327712 | tf_op jit(solution)/shard_map/ppermute | solution.py:363
  167.8 2.3 %collective-permute-start.7 = (bf16[6,128,128]{2,1,0:T(8,128)(2,1)S(1)}, bf16[6,128,128]{2,1,0:T(8,128)(2,1)S(1)}, u32[]{:S(2)}, u32[]{:S(2)}) collective-permute-start(bf16[6,128,128]{2,1,0:T(8,128)(2,1)S(1)} %get-tuple-element.64), channel_id=1, source_target_pairs={{0,96},{8,104},{16,112},{24,120},{32,64},{40,72},{48,80},{56,88},{... | collective-permute-start | bytes 589832 | tf_op jit(solution)/shard_map/ppermute | solution.py:363
  171.4 1.4 collective-permute-start.9
  172.8 2.7 %collective-permute-done.19.refs_11_ = bf16[5,128,128]{2,1,0:T(8,128)(2,1)S(1)} collective-permute-done((bf16[5,128,128]{2,1,0:T(8,128)(2,1)S(1)}, bf16[5,128,128]{2,1,0:T(8,128)(2,1)S(1)}, u32[]{:S(2)}, u32[]{:S(2)}) %collective-permute-start.19) | collective-permute-done | bytes 163872 | tf_op jit(solution)/shard_map/ppermute | solution.py:363
  177.2 2.5 %finish.1 = f32[32,128,128]{2,1,0:T(8,128)} custom-call(s32[1]{0:T(128)} %bitcast.me_ref, s32[1]{0:T(128)S(6)} %copy.14.count_ref, s32[16,128]{1,0:T(8,128)S(1)} %get-tuple-element.46.refs_2_.table_ref, bf16[6,128,128]{2,1,0:T(8,128)(2,1)S(1)} %get-tuple-element.63.refs_0_, bf16[6,128,128]{2,1,0:T(8,128)(2,1)S(1)} %collective-permute-done.7.refs_1_, ...), custom_call_target="tpu_custom_call" | custom-call | tf_op jit(solution)/shard_map/finish/pallas_call | solution.py:343
  (51 shorter events, 12.1 us)
Async XLA Ops:
  18.4 4.0 %copy-start.5 = (bf16[320,16384]{1,0:T(8,128)(2,1)S(1)}, bf16[320,16384]{1,0:T(8,128)(2,1)}, u32[]{:S(2)}) copy-start(bf16[320,16384]{1,0:T(8,128)(2,1)} %em_ref.3) | copy-start | bytes 31457284
  25.7 3.8 %copy-start.10 = (f32[320]{0:T(512)S(1)}, f32[320]{0:T(512)}, u32[]{:S(2)}) copy-start(f32[320]{0:T(512)} %param.9) | copy-start | bytes 3844
  25.7 34.6 %all-to-all-start.1 = ((bf16[32,320,128]{2,1,0:T(8,128)(2,1)}), bf16[32,320,128]{2,1,0:T(8,128)(2,1)S(1)}, u32[]{:S(2)}, u32[]{:S(2)}) async-start(bf16[32,320,128]{2,1,0:T(8,128)(2,1)} %copy-done.7), calls=%async_computation.1 | async-start | bytes 5242880 | tf_op jit(solution)/shard_map/all_to_all | solution.py:379
  29.6 4.0 %copy-start.6 = (bf16[320,16384]{1,0:T(8,128)(2,1)S(1)}, bf16[320,16384]{1,0:T(8,128)(2,1)}, u32[]{:S(2)}) copy-start(bf16[320,16384]{1,0:T(8,128)(2,1)} %adj_ref.1) | copy-start | bytes 31457284
  33.6 26.7 %copy-start.8 = (s32[24]{0:T(128)S(1)}, s32[24]{0:T(128)}, u32[]{:S(2)}) copy-start(s32[24]{0:T(128)} %constant.18.clone.refs_1_) | copy-start | bytes 292
  46.3 4.5 %copy-start = (bf16[128,128,384]{2,1,0:T(8,128)(2,1)}, bf16[128,128,384]{2,1,0:T(8,128)(2,1)S(1)}, u32[]{:S(2)}) copy-start(bf16[128,128,384]{2,1,0:T(8,128)(2,1)S(1)} %get-tuple-element.49.refs_3_) | copy-start | bytes 37748740
  50.8 4.5 %copy-start.2 = (bf16[128,384,128]{2,1,0:T(8,128)(2,1)}, bf16[128,384,128]{2,1,0:T(8,128)(2,1)S(1)}, u32[]{:S(2)}) copy-start(bf16[128,384,128]{2,1,0:T(8,128)(2,1)S(1)} %get-tuple-element.50.refs_4_) | copy-start | bytes 37748740
  60.2 25.9 %copy-start.4 = (bf16[32,320,128]{2,1,0:T(8,128)(2,1)}, bf16[32,320,128]{2,1,0:T(8,128)(2,1)S(1)}, u32[]{:S(2)}) copy-start(bf16[32,320,128]{2,1,0:T(8,128)(2,1)S(1)} %all-to-all-done.1.refs_5_) | copy-start | bytes 7864324
  60.2 5.5 %copy-start.1 = (bf16[128,128,384]{2,1,0:T(8,128)(2,1)S(1)}, bf16[128,128,384]{2,1,0:T(8,128)(2,1)}, u32[]{:S(2)}) copy-start(bf16[128,128,384]{2,1,0:T(8,128)(2,1)} %copy-done) | copy-start | bytes 37748740
  65.8 4.6 %copy-start.3 = (bf16[128,384,128]{2,1,0:T(8,128)(2,1)S(1)}, bf16[128,384,128]{2,1,0:T(8,128)(2,1)}, u32[]{:S(2)}) copy-start(bf16[128,384,128]{2,1,0:T(8,128)(2,1)} %copy-done.2) | copy-start | bytes 37748740
  86.1 11.7 %copy-start.11 = (s32[24]{0:T(128)S(1)}, s32[24]{0:T(128)}, u32[]{:S(2)}) copy-start(s32[24]{0:T(128)} %constant.17.clone) | copy-start | bytes 292
  86.1 11.7 %collective-permute-start.10 = (bf16[128,128,128]{2,1,0:T(8,128)(2,1)}, bf16[128,128,128]{2,1,0:T(8,128)(2,1)}, u32[]{:S(2)}, u32[]{:S(2)}) collective-permute-start(bf16[128,128,128]{2,1,0:T(8,128)(2,1)} %tiles.6), channel_id=1, source_target_pairs={{0,8},{8,0},{16,24},{24,16},{32,40},{40,32},{48,56},{56,48},{64,72... | collective-permute-start | bytes 12582920 | tf_op jit(solution)/shard_map/ppermute | solution.py:363
  97.2 21.3 %collective-permute-start = (bf16[128,128,128]{2,1,0:T(8,128)(2,1)}, bf16[128,128,128]{2,1,0:T(8,128)(2,1)S(1)}, u32[]{:S(2)}, u32[]{:S(2)}) collective-permute-start(bf16[128,128,128]{2,1,0:T(8,128)(2,1)} %tiles.4), channel_id=1, source_target_pairs={{0,8},{8,0},{16,24},{24,16},{32,40},{40,32},{48,56},{56,48},{64,72... | collective-permute-start | bytes 12582920 | tf_op jit(solution)/shard_map/ppermute | solution.py:363
  114.1 20.4 %collective-permute-start.12 = (bf16[20,128,128]{2,1,0:T(8,128)(2,1)S(1)}, bf16[20,128,128]{2,1,0:T(8,128)(2,1)S(1)}, u32[]{:S(2)}, u32[]{:S(2)}) collective-permute-start(bf16[20,128,128]{2,1,0:T(8,128)(2,1)S(1)} %get-tuple-element.72), channel_id=1, source_target_pairs={{0,32},{8,40},{16,48},{24,56},{32,0},{40,8},{48,16},{56,24},{64,96... | collective-permute-start | bytes 1966088 | tf_op jit(solution)/shard_map/ppermute | solution.py:363
  115.7 19.9 %collective-permute-start.11 = (bf16[24,128,128]{2,1,0:T(8,128)(2,1)S(1)}, bf16[24,128,128]{2,1,0:T(8,128)(2,1)S(1)}, u32[]{:S(2)}, u32[]{:S(2)}) collective-permute-start(bf16[24,128,128]{2,1,0:T(8,128)(2,1)S(1)} %get-tuple-element.70), channel_id=1, source_target_pairs={{0,16},{8,24},{16,0},{24,8},{32,48},{40,56},{48,32},{56,40},{64,80... | collective-permute-start | bytes 2359304 | tf_op jit(solution)/shard_map/ppermute | solution.py:363
  116.3 18.7 %collective-permute-start.13 = (bf16[20,128,128]{2,1,0:T(8,128)(2,1)S(1)}, bf16[20,128,128]{2,1,0:T(8,128)(2,1)S(1)}, u32[]{:S(2)}, u32[]{:S(2)}) collective-permute-start(bf16[20,128,128]{2,1,0:T(8,128)(2,1)S(1)} %get-tuple-element.74), channel_id=1, source_target_pairs={{0,96},{8,104},{16,112},{24,120},{32,64},{40,72},{48,80},{56,88},{... | collective-permute-start | bytes 1966088 | tf_op jit(solution)/shard_map/ppermute | solution.py:363
  118.5 2.0 %copy-start.9 = (bf16[128,128,128]{2,1,0:T(8,128)(2,1)}, bf16[128,128,128]{2,1,0:T(8,128)(2,1)S(1)}, u32[]{:S(2)}) copy-start(bf16[128,128,128]{2,1,0:T(8,128)(2,1)S(1)} %collective-permute-done.refs_6_) | copy-start | bytes 12582916
  132.1 21.2 %collective-permute-start.1 = (bf16[24,128,128]{2,1,0:T(8,128)(2,1)S(1)}, bf16[24,128,128]{2,1,0:T(8,128)(2,1)S(1)}, u32[]{:S(2)}, u32[]{:S(2)}) collective-permute-start(bf16[24,128,128]{2,1,0:T(8,128)(2,1)S(1)} %get-tuple-element.52), channel_id=1, source_target_pairs={{0,16},{8,24},{16,0},{24,8},{32,48},{40,56},{48,32},{56,40},{64,80... | collective-permute-start | bytes 2359304 | tf_op jit(solution)/shard_map/ppermute | solution.py:363
  133.8 17.7 %collective-permute-start.2 = (bf16[20,128,128]{2,1,0:T(8,128)(2,1)S(1)}, bf16[20,128,128]{2,1,0:T(8,128)(2,1)S(1)}, u32[]{:S(2)}, u32[]{:S(2)}) collective-permute-start(bf16[20,128,128]{2,1,0:T(8,128)(2,1)S(1)} %get-tuple-element.54), channel_id=1, source_target_pairs={{0,32},{8,40},{16,48},{24,56},{32,0},{40,8},{48,16},{56,24},{64,96... | collective-permute-start | bytes 1966088 | tf_op jit(solution)/shard_map/ppermute | solution.py:363
  134.4 18.9 %collective-permute-start.3 = (bf16[20,128,128]{2,1,0:T(8,128)(2,1)S(1)}, bf16[20,128,128]{2,1,0:T(8,128)(2,1)S(1)}, u32[]{:S(2)}, u32[]{:S(2)}) collective-permute-start(bf16[20,128,128]{2,1,0:T(8,128)(2,1)S(1)} %get-tuple-element.56), channel_id=1, source_target_pairs={{0,96},{8,104},{16,112},{24,120},{32,64},{40,72},{48,80},{56,88},{... | collective-permute-start | bytes 1966088 | tf_op jit(solution)/shard_map/ppermute | solution.py:363
  136.2 24.1 %collective-permute-start.15 = (bf16[10,128,128]{2,1,0:T(8,128)(2,1)S(1)}, bf16[10,128,128]{2,1,0:T(8,128)(2,1)S(1)}, u32[]{:S(2)}, u32[]{:S(2)}) collective-permute-start(bf16[10,128,128]{2,1,0:T(8,128)(2,1)S(1)} %get-tuple-element.78), channel_id=1, source_target_pairs={{0,96},{8,104},{16,112},{24,120},{32,64},{40,72},{48,80},{56,88},{... | collective-permute-start | bytes 983048 | tf_op jit(solution)/shard_map/ppermute | solution.py:363
  139.0 22.0 %collective-permute-start.14 = (bf16[12,128,128]{2,1,0:T(8,128)(2,1)S(1)}, bf16[12,128,128]{2,1,0:T(8,128)(2,1)S(1)}, u32[]{:S(2)}, u32[]{:S(2)}) collective-permute-start(bf16[12,128,128]{2,1,0:T(8,128)(2,1)S(1)} %get-tuple-element.76), channel_id=1, source_target_pairs={{0,32},{8,40},{16,48},{24,56},{32,0},{40,8},{48,16},{56,24},{64,96... | collective-permute-start | bytes 1179656 | tf_op jit(solution)/shard_map/ppermute | solution.py:363
  151.4 9.5 %collective-permute-start.16 = (bf16[10,128,128]{2,1,0:T(8,128)(2,1)S(1)}, bf16[10,128,128]{2,1,0:T(8,128)(2,1)S(1)}, u32[]{:S(2)}, u32[]{:S(2)}) collective-permute-start(bf16[10,128,128]{2,1,0:T(8,128)(2,1)S(1)} %get-tuple-element.80), channel_id=1, source_target_pairs={{0,16},{8,24},{16,0},{24,8},{32,48},{40,56},{48,32},{56,40},{64,80... | collective-permute-start | bytes 983048 | tf_op jit(solution)/shard_map/ppermute | solution.py:363
  153.9 13.7 %collective-permute-start.4 = (bf16[12,128,128]{2,1,0:T(8,128)(2,1)S(1)}, bf16[12,128,128]{2,1,0:T(8,128)(2,1)S(1)}, u32[]{:S(2)}, u32[]{:S(2)}) collective-permute-start(bf16[12,128,128]{2,1,0:T(8,128)(2,1)S(1)} %get-tuple-element.58), channel_id=1, source_target_pairs={{0,32},{8,40},{16,48},{24,56},{32,0},{40,8},{48,16},{56,24},{64,96... | collective-permute-start | bytes 1179656 | tf_op jit(solution)/shard_map/ppermute | solution.py:363
  154.1 13.0 %collective-permute-start.5 = (bf16[10,128,128]{2,1,0:T(8,128)(2,1)S(1)}, bf16[10,128,128]{2,1,0:T(8,128)(2,1)S(1)}, u32[]{:S(2)}, u32[]{:S(2)}) collective-permute-start(bf16[10,128,128]{2,1,0:T(8,128)(2,1)S(1)} %get-tuple-element.60), channel_id=1, source_target_pairs={{0,96},{8,104},{16,112},{24,120},{32,64},{40,72},{48,80},{56,88},{... | collective-permute-start | bytes 983048 | tf_op jit(solution)/shard_map/ppermute | solution.py:363
  160.3 7.2 %collective-permute-start.6 = (bf16[10,128,128]{2,1,0:T(8,128)(2,1)S(1)}, bf16[10,128,128]{2,1,0:T(8,128)(2,1)S(1)}, u32[]{:S(2)}, u32[]{:S(2)}) collective-permute-start(bf16[10,128,128]{2,1,0:T(8,128)(2,1)S(1)} %get-tuple-element.62), channel_id=1, source_target_pairs={{0,16},{8,24},{16,0},{24,8},{32,48},{40,56},{48,32},{56,40},{64,80... | collective-permute-start | bytes 983048 | tf_op jit(solution)/shard_map/ppermute | solution.py:363
  161.2 10.2 %collective-permute-start.18 = (bf16[5,128,128]{2,1,0:T(8,128)(2,1)S(1)}, bf16[5,128,128]{2,1,0:T(8,128)(2,1)S(1)}, u32[]{:S(2)}, u32[]{:S(2)}) collective-permute-start(bf16[5,128,128]{2,1,0:T(8,128)(2,1)S(1)} %get-tuple-element.84), channel_id=1, source_target_pairs={{0,16},{8,24},{16,0},{24,8},{32,48},{40,56},{48,32},{56,40},{64,80... | collective-permute-start | bytes 491528 | tf_op jit(solution)/shard_map/ppermute | solution.py:363
  162.7 14.5 %collective-permute-start.17 = (bf16[6,128,128]{2,1,0:T(8,128)(2,1)S(1)}, bf16[6,128,128]{2,1,0:T(8,128)(2,1)S(1)}, u32[]{:S(2)}, u32[]{:S(2)}) collective-permute-start(bf16[6,128,128]{2,1,0:T(8,128)(2,1)S(1)} %get-tuple-element.82), channel_id=1, source_target_pairs={{0,96},{8,104},{16,112},{24,120},{32,64},{40,72},{48,80},{56,88},{... | collective-permute-start | bytes 589832 | tf_op jit(solution)/shard_map/ppermute | solution.py:363
  167.8 9.4 %collective-permute-start.7 = (bf16[6,128,128]{2,1,0:T(8,128)(2,1)S(1)}, bf16[6,128,128]{2,1,0:T(8,128)(2,1)S(1)}, u32[]{:S(2)}, u32[]{:S(2)}) collective-permute-start(bf16[6,128,128]{2,1,0:T(8,128)(2,1)S(1)} %get-tuple-element.64), channel_id=1, source_target_pairs={{0,96},{8,104},{16,112},{24,120},{32,64},{40,72},{48,80},{56,88},{... | collective-permute-start | bytes 589832 | tf_op jit(solution)/shard_map/ppermute | solution.py:363
  170.1 5.3 %collective-permute-start.19 = (bf16[5,128,128]{2,1,0:T(8,128)(2,1)S(1)}, bf16[5,128,128]{2,1,0:T(8,128)(2,1)S(1)}, u32[]{:S(2)}, u32[]{:S(2)}) collective-permute-start(bf16[5,128,128]{2,1,0:T(8,128)(2,1)S(1)} %get-tuple-element.86), channel_id=1, source_target_pairs={{0,32},{8,40},{16,48},{24,56},{32,0},{40,8},{48,16},{56,24},{64,96... | collective-permute-start | bytes 491528 | tf_op jit(solution)/shard_map/ppermute | solution.py:363
  170.8 5.3 %collective-permute-start.8 = (bf16[5,128,128]{2,1,0:T(8,128)(2,1)S(1)}, bf16[5,128,128]{2,1,0:T(8,128)(2,1)S(1)}, u32[]{:S(2)}, u32[]{:S(2)}) collective-permute-start(bf16[5,128,128]{2,1,0:T(8,128)(2,1)S(1)} %get-tuple-element.66), channel_id=1, source_target_pairs={{0,16},{8,24},{16,0},{24,8},{32,48},{40,56},{48,32},{56,40},{64,80... | collective-permute-start | bytes 491528 | tf_op jit(solution)/shard_map/ppermute | solution.py:363
  171.4 5.8 %collective-permute-start.9 = (bf16[5,128,128]{2,1,0:T(8,128)(2,1)S(1)}, bf16[5,128,128]{2,1,0:T(8,128)(2,1)S(1)}, u32[]{:S(2)}, u32[]{:S(2)}) collective-permute-start(bf16[5,128,128]{2,1,0:T(8,128)(2,1)S(1)} %get-tuple-element.68), channel_id=1, source_target_pairs={{0,32},{8,40},{16,48},{24,56},{32,0},{40,8},{48,16},{56,24},{64,96... | collective-permute-start | bytes 491528 | tf_op jit(solution)/shard_map/ppermute | solution.py:363
  (1 other events, 1.5 us)
